TPU v7x, 32 devices: a whole 2x2x4 slice. The times are simulated.
32 devices in a mesh: section: 8 (over y, x, core), head: 4 (over z).
Axes of the slice: x: 2, y: 2, z: 4, core: 2. Of those that a mesh axis runs over, the one named last changes fastest.
Arguments:
- residual: bfloat16 [2048, 2, 4096], P(('section', 'head')), may hold values from -3 to 3
- queries: bfloat16 [2, 2048, 4096], P(None, 'section', 'head'), may hold values from -80 to 80
- new_kv: bfloat16 [2, 2, 2048, 1024], P(None, None, 'section'), may hold values from -6 to 6
- cache_kv: bfloat16 [2, 12288, 1024], P(None, 'section'), may hold values from -6 to 6
- lengths: int32 [8], replicated, may hold values from 1 to 1536, as said below
- out_weight: bfloat16 [8, 4096, 4096], P('section', 'head'), may hold values from -0.09375 to 0.09375
Outputs:
- advanced: bfloat16 [2048, 2, 4096], P(('section', 'head'))
Inputs may be any that keep to these rules, and one draw needn't show every extreme that they name: `lengths`: some section's cache holds 1536 positions while the section half the sections away holds at most 128.
All inputs are finite; a program needn't handle non-finite values.
Results may differ from a plain program's by a relative error of at most 0.013.
Values may be sent and summed in bfloat16 or wider, within the bound.
No kernel may reach another device: no remote copies, remote signals or barrier semaphores. Data moves between devices by JAX's collectives and lax.ppermute only.
A program may use at most 64 MiB of HBM per device.

v0:
```python
import math

import jax
import jax.numpy as jnp
from jax import lax
from jax.sharding import PartitionSpec as P

QH = 32
KVH = 8
HD = 128
BLK = 128


neg_large = -1e30


def shifted(block, axis, distance):
    devices = range(lax.axis_size(axis))
    route = [((i - distance) % len(devices), i) for i in devices]
    return lax.ppermute(block, axis, route)


def attend_block(partial_state, query_rows, key_rows, value_rows, visible):
    running, denominator, numerator = partial_state
    scores = jnp.einsum(
        "grd,gkd->grk", query_rows, key_rows, preferred_element_type=jnp.float32
    ) * (1.0 / math.sqrt(HD))
    scores = jnp.where(visible, scores, neg_large)
    highest = jnp.maximum(running, jnp.max(scores, axis=-1))
    weights = jnp.where(visible, jnp.exp(scores - highest[..., None]), 0.0)
    factor = jnp.exp(running - highest)
    denominator = denominator * factor + jnp.sum(weights, axis=-1)
    rounded = weights.astype(jnp.bfloat16)
    numerator = numerator * factor[..., None] + jnp.einsum(
        "grk,gkd->grd", rounded, value_rows, preferred_element_type=jnp.float32
    )
    return (highest, denominator, numerator)


def attend_range(
    partial_state,
    query_rows,
    key_blocks,
    value_blocks,
    first_block,
    block_count,
    offset,
    length_now,
):

    def one_block(block_index, state_now):
        start_row = (first_block + block_index) * BLK
        key_rows = lax.dynamic_slice_in_dim(key_blocks, start_row, BLK, 1)
        value_rows = lax.dynamic_slice_in_dim(value_blocks, start_row, BLK, 1)
        position = offset + start_row + jnp.arange(BLK, dtype=jnp.int32)
        visible = (position < length_now)[None, None, :]
        return attend_block(state_now, query_rows, key_rows, value_rows, visible)

    return lax.fori_loop(0, block_count, one_block, partial_state)


def project_rows(block_heads, weight_rows):
    return jnp.dot(block_heads, weight_rows, preferred_element_type=jnp.float32)


def on_device(residual, queries, new_kv, cache_kv, lengths, out_weight):
    section_index = lax.axis_index("section")
    head_index = lax.axis_index("head")
    tick_count, row_count, head_width = queries.shape
    heads_here = head_width // HD
    group_size = QH // KVH
    kv_count = max(1, heads_here // group_size)
    inner_count = min(heads_here, group_size)
    kv_width = kv_count * HD
    kv_first = head_index * heads_here // group_size
    capacity = cache_kv.shape[1]
    cache_part = lax.dynamic_slice_in_dim(cache_kv, kv_first * HD, kv_width, 2)
    cache_heads = cache_part.reshape(2, capacity, kv_count, HD).transpose(0, 2, 1, 3)
    fresh = lax.dynamic_slice_in_dim(new_kv, kv_first * HD, kv_width, 3)
    fresh = fresh.reshape(tick_count, 2, row_count, kv_count, HD).transpose(0, 1, 3, 2, 4)
    query_rows = queries.reshape(tick_count, row_count, kv_count, inner_count, HD).transpose(
        2, 0, 3, 1, 4
    )
    all_rows = tick_count * inner_count * row_count
    query_rows = query_rows.reshape(kv_count, all_rows, HD)
    my_length = lengths[section_index]
    my_blocks = (my_length + BLK - 1) // BLK
    empty_state = (
        jnp.full((kv_count, all_rows), neg_large, jnp.float32),
        jnp.zeros((kv_count, all_rows), jnp.float32),
        jnp.zeros((kv_count, all_rows, HD), jnp.float32),
    )
    own_state = attend_range(
        empty_state, query_rows, cache_heads[0], cache_heads[1], 0, my_blocks, 0, my_length
    )
    tick_rows = inner_count * row_count
    running_ticks = own_state[0].reshape(kv_count, tick_count, tick_rows)
    denominator_ticks = own_state[1].reshape(kv_count, tick_count, tick_rows)
    numerator_ticks = own_state[2].reshape(kv_count, tick_count, tick_rows, HD)
    query_ticks = query_rows.reshape(kv_count, tick_count, tick_rows, HD)
    query_position = jnp.arange(tick_rows, dtype=jnp.int32) % row_count
    causal = (jnp.arange(row_count, dtype=jnp.int32)[None, :] <= query_position[:, None])[None]
    everything = jnp.ones((1, 1, row_count), jnp.bool_)
    head_blocks = []
    for tick_now in range(tick_count):
        state_now = (
            running_ticks[:, tick_now],
            denominator_ticks[:, tick_now],
            numerator_ticks[:, tick_now],
        )
        for earlier in range(tick_now + 1):
            mask_now = causal if earlier == tick_now else everything
            state_now = attend_block(
                state_now, query_ticks[:, tick_now], fresh[earlier, 0], fresh[earlier, 1], mask_now
            )
        mixed = state_now[2] / state_now[1][..., None]
        mixed = mixed.reshape(kv_count, inner_count, row_count, HD).transpose(2, 0, 1, 3)
        head_blocks.append(mixed.reshape(row_count, head_width).astype(jnp.bfloat16))
    weight_rows = out_weight[0]
    pieces = []
    for tick_now in range(tick_count):
        pieces.append(
            lax.psum_scatter(
                project_rows(head_blocks[tick_now], weight_rows).astype(jnp.bfloat16),
                "head",
                scatter_dimension=0,
                tiled=True,
            ).astype(jnp.float32)
        )
    projected = jnp.stack(pieces, axis=1)
    updated = (residual.astype(jnp.float32) + projected).astype(jnp.bfloat16)
    return shifted(updated, "section", 1)


def solution(mesh):
    placed = (
        P(("section", "head"), None, None),
        P(None, "section", "head"),
        P(None, None, "section", None),
        P(None, "section", None),
        P(),
        P("section", "head", None),
    )
    return jax.shard_map(
        on_device,
        mesh=mesh,
        in_specs=placed,
        out_specs=P(("section", "head"), None, None),
        check_vma=False,
    )
```

profile of v0, /device:TPU:16, one launch (start us, length us, event | category | flops | bytes accessed | tf_op | source)
XLA Modules:
  0.0 230.2 jit_solution(17853840920643844391)
XLA Ops:
  6.5 1.4 dynamic_slice.15
  8.5 2.6 %reshape.152 = bf16[2,256,2,4,128]{4,3,2,1,0:T(4,128)(2,1)} reshape(bf16[2,256,1024]{2,1,0:T(8,128)(2,1)} %param.9) | data formatting | bytes 2097152 | tf_op jit(solution)/shard_map/reshape | solution.py:81
  11.0 1.5 copy.44
  13.7 2.7 %constant_dynamic-slice_fusion.1 = bf16[2,1536,256]{2,1,0:T(8,128)(2,1)} fusion(bf16[2,1536,1024]{2,1,0:T(8,128)(2,1)} %param.11, s32[]{:T(128)S(6)} %select_n.64), kind=kLoop, calls=%fused_computation.97 | loop fusion | bytes 3145732 | tf_op jit(solution)/shard_map/dynamic_slice | solution.py:77
  16.4 2.6 %copy.47 = bf16[2,1536,256]{1,2,0:T(8,128)(2,1)} copy(bf16[2,1536,256]{2,1,0:T(8,128)(2,1)} %constant_dynamic-slice_fusion.1) | data formatting | bytes 3145728
  19.0 2.6 %slice_bitcast_fusion.2 = (bf16[2,1536,128]{1,2,0:T(8,128)(2,1)}, bf16[2,1536,128]{1,2,0:T(8,128)(2,1)}) fusion(bf16[2,2,1536,128]{2,3,1,0:T(8,128)(2,1)} %bitcast.162), kind=kLoop, calls=%fused_computation.65 | loop fusion | bytes 3145728 | tf_op jit(solution)/shard_map/squeeze | solution.py:94
  21.6 1.5 broadcast_in_dim.90
  23.1 24.7 %while.14 = (s32[]{:T(128)}, f32[2,2048]{1,0:T(2,128)S(1)}, f32[2,2048]{1,0:T(2,128)S(1)}, f32[2,2048,128]{2,1,0:T(8,128)}, s32[]{:T(128)}, /*index=5*/s32[]{:T(...) while((s32[]{:T(128)}, f32[2,2048]{1,0:T(2,128)S(1)}, ...), condition=%wide.region_3.4_spmd, body=%wide.region_0.3_spmd.sunk | while | flops 274211072 | bytes 28705524 | solution.py:59
  23.7 1.6 fusion.89
  25.7 2.2 convolution_add_fusion.5
  27.9 1.3 copy-done.2
  29.8 1.6 fusion.89
  31.9 2.2 convolution_add_fusion.5
  34.1 1.3 copy-done.2
  36.0 1.6 fusion.89
  38.1 2.2 convolution_add_fusion.5
  40.3 1.3 copy-done.2
  42.2 1.6 fusion.89
  44.2 2.2 convolution_add_fusion.5
  46.5 1.3 copy-done.2
  48.7 2.1 copy.49
  50.8 2.1 copy.29
  53.0 1.4 bitcast_reduce_fusion
  58.5 1.4 fusion.35
  60.1 7.1 %fusion.17 = bf16[256,4096]{1,0:T(8,128)(2,1)} fusion(bf16[256,1024]{0,1:T(8,128)(2,1)S(1)} %bitcast.166, bf16[1,1024,4096]{2,1,0:T(8,128)(2,1)} %param.13), kind=kOutput, calls=%fused_computation.22 | convolution fusion | flops 2148532224 | bytes 11010048 | tf_op jit(solution)/shard_map/dot_general | solution.py:63
  68.3 3.0 %fusion.33 = f32[2,1024,128]{2,1,0:T(8,128)S(1)} fusion(f32[2,256,1024]{2,1,0:T(8,128)} %copy-done.4, f32[2,2,1024,128]{3,2,1,0:T(8,128)} %bitcast.159, f32[2,1024]{1,0:T(2,128)S(1)} %get-tuple-element.95, f32[2,1024]{1,0:T(2,128)S(1)} %get-tuple-element.101, f32[2,1024]{1,0:T(2,128)S(1)} %get-tuple-element.102, bf16[2,2,2,256,128]{4,3,2,1,0:T(8,128)(2,1)S(1)} %bitcast.176), kind=kOutput, calls=%fused_computation.43 | convolution fusion | flops 136577024 | bytes 4349952 | tf_op jit(solution)/shard_map/grk,gkd->grd/dot_general | solution.py:34
  72.5 7.1 %fusion.20 = bf16[256,4096]{1,0:T(8,128)(2,1)} fusion(bf16[256,1024]{0,1:T(8,128)(2,1)S(1)} %bitcast.167, bf16[1,1024,4096]{2,1,0:T(8,128)(2,1)} %param.13), kind=kOutput, calls=%fused_computation.23 | convolution fusion | flops 2148532224 | bytes 11010048 | tf_op jit(solution)/shard_map/dot_general | solution.py:63
  79.6 79.0 %reduce-scatter.3.cloned.1.call-done = bf16[64,4096]{1,0:T(8,128)(2,1)} async-done(((bf16[256,4096]{1,0:T(8,128)(2,1)}), bf16[64,4096]{1,0:T(8,128)(2,1)}) %reduce-scatter.3.cloned.1.call-update) | async-done | bytes 524304 | tf_op jit(solution)/shard_map/reduce_scatter | solution.py:123
  158.7 45.6 %reduce-scatter.5.cloned.1.call-done = bf16[64,4096]{1,0:T(8,128)(2,1)} async-done(((bf16[256,4096]{1,0:T(8,128)(2,1)}), bf16[64,4096]{1,0:T(8,128)(2,1)}) %reduce-scatter.5.cloned.1.call-update) | async-done | bytes 524304 | tf_op jit(solution)/shard_map/reduce_scatter | solution.py:123
  204.3 1.9 add_convert_fusion
  206.2 15.1 %collective-permute-done = bf16[64,2,4096]{2,0,1:T(8,128)(2,1)S(1)} collective-permute-done((bf16[64,2,4096]{2,0,1:T(8,128)(2,1)S(1)}, bf16[64,2,4096]{2,0,1:T(8,128)(2,1)S(1)}, u32[]{:S(2)}, u32[]{:S(2)}) %collective-permute-start) | collective-permute-done | bytes 1048608 | tf_op jit(solution)/shard_map/ppermute | solution.py:20
  221.3 2.1 copy.39
  (72 shorter events, 12.9 us)
Async XLA Ops:
  6.5 41.3 %copy-start = (bf16[2,2,256,1024]{3,2,1,0:T(8,128)(2,1)S(1)}, bf16[2,2,256,1024]{3,2,1,0:T(8,128)(2,1)}, u32[]{:S(2)}) copy-start(bf16[2,2,256,1024]{3,2,1,0:T(8,128)(2,1)} %param.10) | copy-start | bytes 6291460
  6.5 152.1 %reduce-scatter.3.cloned.1.call-start = ((), (), s32[]{:S(2)}) async-start(), calls=%async_computation.2 | async-start | bytes 2621440 | tf_op jit(solution)/shard_map/reduce_scatter | solution.py:123
  11.0 1.5 copy-start.5
  23.7 2.0 copy-start.1
  27.9 1.3 copy-start.2
  29.8 2.0 copy-start.1
  34.1 1.3 copy-start.2
  36.0 2.0 copy-start.1
  40.3 1.3 copy-start.2
  42.2 2.0 copy-start.1
  46.5 1.3 copy-start.2
  47.8 5.2 %copy-start.6 = (bf16[2,256,2,4,128]{4,1,3,2,0:T(8,128)(2,1)S(1)}, bf16[2,256,2,4,128]{4,1,3,2,0:T(8,128)(2,1)}, u32[]{:S(2)}) copy-start(bf16[2,256,2,4,128]{4,1,3,2,0:T(8,128)(2,1)} %copy.22) | copy-start | bytes 3145732
  52.9 1.5 copy-start.9
  54.4 1.7 copy-start.4
  56.1 1.3 copy-start.7
  56.1 2.3 %copy-start.3 = (f32[2,2048,128]{2,1,0:T(8,128)S(1)}, f32[2,2048,128]{2,1,0:T(8,128)}, u32[]{:S(2)}) copy-start(f32[2,2048,128]{2,1,0:T(8,128)} %get-tuple-element.55) | copy-start | bytes 6291460
  67.2 1.0 copy-start.10
  67.2 137.0 %reduce-scatter.5.cloned.1.call-start = ((), (), s32[]{:S(2)}) async-start(), calls=%async_computation.3 | async-start | bytes 2621440 | tf_op jit(solution)/shard_map/reduce_scatter | solution.py:123
  68.3 3.0 %copy-start.8 = (f32[2,256,1024]{2,1,0:T(8,128)S(1)}, f32[2,256,1024]{2,1,0:T(8,128)}, u32[]{:S(2)}) copy-start(f32[2,256,1024]{2,1,0:T(8,128)} %copy-done.7) | copy-start | bytes 6291460
  79.6 124.7 %copy-start.11 = (bf16[64,2,4096]{2,1,0:T(2,128)(2,1)S(1)}, bf16[64,2,4096]{2,1,0:T(2,128)(2,1)}, u32[]{:S(2)}) copy-start(bf16[64,2,4096]{2,1,0:T(2,128)(2,1)} %param.8) | copy-start | bytes 3145732
  206.1 15.2 %collective-permute-start = (bf16[64,2,4096]{2,0,1:T(8,128)(2,1)S(1)}, bf16[64,2,4096]{2,0,1:T(8,128)(2,1)S(1)}, u32[]{:S(2)}, u32[]{:S(2)}) collective-permute-start(bf16[64,2,4096]{2,0,1:T(8,128)(2,1)S(1)} %add_convert_fusion), channel_id=1, source_target_pairs={{28,0},{0,4},{4,8},{8,12},{12,16},{16,20},{20,24},{24,28},{29,1},{... | collective-permute-start | bytes 3145736 | tf_op jit(solution)/shard_map/ppermute | solution.py:20
Sparse Core Ops, SparseCore 0:
  67.4 91.2 reduce-scatter.2
  161.0 43.1 reduce-scatter.4
where the time goes:
time: 234 us; the launch traced here: 230 us
  waiting for transfers between devices  140 us (60%)
  matrix products  37.7 us (16%)
  local copies, waits for them, and re-layouts  31.1 us (13%)
  between operations  14.1 us (6%)
  other arithmetic  7.04 us (3%)
    reduce_scatter x2, waiting for transfers between devices, on_device(): lax.psum_scatter(project_rows(head_blocks[tick_now], weight_rows).astype(...  125 us
    ppermute x1, waiting for transfers between devices, shifted(): return lax.ppermute(block, axis, route)  15.1 us
    dot_general x7, matrix products, attend_block(): jnp.einsum('grk,gkd->grd', rounded, value_rows, preferred_element_type=jn...  14.3 us
    dot_general x2, matrix products, project_rows(): return jnp.dot(block_heads, weight_rows, preferred_element_type=jnp.float32)  14.2 us
    dot_general x7, matrix products, attend_block(): jnp.einsum('grd,gkd->grk', query_rows, key_rows, preferred_element_type=j...  9.22 us
    unnamed x22, local copies, waits for them, and re-layouts  6.91 us
    while x20, local copies, waits for them, and re-layouts  5.37 us
  transfers between devices with their start and end apart: 3, of which 3 were waited for; matrix products, arithmetic and copies ran while one was open for 5% of the time, Pallas kernels for 0%

commit v1 on v0

v1 whole, which is shorter than its diff:
```python
import functools
import math

import jax
import jax.numpy as jnp
from jax import lax
from jax.experimental import pallas as pl
from jax.experimental.pallas import tpu as pltpu
from jax.sharding import PartitionSpec as P

QH = 32
KVH = 8
HD = 128
GROUP = QH // KVH
KEY_BLOCK = 512
COLUMN_TILE = 512

neg_large = -1e30
EXPONENT = math.log2(math.e) / math.sqrt(HD)


def rows_kernel(
    ticks,
    rows,
    dep_count,
    place,
    queries,
    new_kv,
    cache_kv,
    out_weight,
    *rest,
):
    out = rest[dep_count]
    q_buf, fresh_buf, cache_buf, w_buf, heads_buf, acc_buf, in_sem, w_sem = rest[dep_count + 1 :]
    tick_count = len(ticks)
    fresh_count = ticks[-1] + 1
    row_first = pl.multiple_of(place[0], rows)
    my_length = place[1]
    kv_width = cache_buf.shape[2]
    kv_column = pl.multiple_of(place[2], HD)
    capacity = cache_buf.shape[1]
    fresh_rows = fresh_buf.shape[2]
    head_width = q_buf.shape[2]
    heads_here = head_width // HD
    kv_count = kv_width // HD
    inner = heads_here // kv_count
    tile_count = w_buf.shape[0]
    tile_width = w_buf.shape[2]

    copies = []
    for index, tick in enumerate(ticks):
        copies.append((queries.at[tick, pl.ds(row_first, rows), :], q_buf.at[index]))
    for tick in range(fresh_count):
        for part in range(2):
            copies.append(
                (new_kv.at[tick, part, :, pl.ds(kv_column, kv_width)], fresh_buf.at[tick, part])
            )
    for part in range(2):
        copies.append((cache_kv.at[part, :, pl.ds(kv_column, kv_width)], cache_buf.at[part]))
    started = [
        pltpu.make_async_copy(source, target, in_sem.at[index])
        for index, (source, target) in enumerate(copies)
    ]
    for copy in started:
        copy.start()
    w_copies = [
        pltpu.make_async_copy(
            out_weight.at[0, :, pl.ds(tile * tile_width, tile_width)], w_buf.at[tile], w_sem.at[tile]
        )
        for tile in range(tile_count)
    ]
    for copy in w_copies:
        copy.start()
    for copy in started:
        copy.wait()

    tick_rows = inner * rows
    all_rows = tick_count * tick_rows
    query_heads = []
    for g in range(kv_count):
        query_heads.append(
            jnp.concatenate(
                [
                    q_buf[index, :, (g * inner + i) * HD : (g * inner + i + 1) * HD]
                    for index in range(tick_count)
                    for i in range(inner)
                ],
                axis=0,
            )
        )

    def one_block(g, state, key_rows, value_rows, visible):
        highest, acc = state
        scores = lax.dot_general(
            query_heads[g], key_rows, (((1,), (1,)), ((), ())), preferred_element_type=jnp.float32
        )
        if visible is not None:
            scores = jnp.where(visible, scores, neg_large)
        now = jnp.maximum(highest, jnp.max(scores, axis=1, keepdims=True))
        weights = jnp.exp2((scores - now) * EXPONENT).astype(jnp.bfloat16)
        wide = jnp.concatenate([value_rows, jnp.ones_like(value_rows)], axis=1)
        added = jnp.dot(weights, wide, preferred_element_type=jnp.float32)
        if acc is not None:
            added = added + acc * jnp.exp2((highest - now) * EXPONENT)
        return now, added

    highest = []
    for g in range(kv_count):
        lanes = slice(g * HD, (g + 1) * HD)
        state = (jnp.full((all_rows, 1), neg_large, jnp.float32), None)
        for earlier in range(fresh_count):
            if tick_count == 1 and earlier < ticks[0]:
                visible = None
            else:
                shape = (all_rows, fresh_rows)
                line = lax.broadcasted_iota(jnp.int32, shape, 0)
                column = lax.broadcasted_iota(jnp.int32, shape, 1)
                position = lax.rem(line, rows) + row_first
                visible = column <= position
                if tick_count > 1:
                    tick_here = line // tick_rows + ticks[0]
                    visible = (tick_here > earlier) | ((tick_here == earlier) & visible)
            state = one_block(
                g,
                state,
                fresh_buf[earlier, 0, :, lanes],
                fresh_buf[earlier, 1, :, lanes],
                visible,
            )
        highest.append(state[0])
        acc_buf[g] = state[1]

    def cache_block(block, carry):
        start = pl.multiple_of(block * KEY_BLOCK, KEY_BLOCK)
        column = lax.broadcasted_iota(jnp.int32, (all_rows, KEY_BLOCK), 1)
        visible = column < my_length - start
        after = []
        for g in range(kv_count):
            lanes = slice(g * HD, (g + 1) * HD)
            now, acc = one_block(
                g,
                (carry[g], acc_buf[g]),
                cache_buf[0, pl.ds(start, KEY_BLOCK), lanes],
                cache_buf[1, pl.ds(start, KEY_BLOCK), lanes],
                visible,
            )
            acc_buf[g] = acc
            after.append(now)
        return tuple(after)

    lax.fori_loop(0, (my_length + KEY_BLOCK - 1) // KEY_BLOCK, cache_block, tuple(highest))

    for g in range(kv_count):
        mixed = (acc_buf[g, :, :HD] / acc_buf[g, :, HD:]).astype(jnp.bfloat16)
        for index in range(tick_count):
            for i in range(inner):
                head = g * inner + i
                first = (index * inner + i) * rows
                heads_buf[index * rows : (index + 1) * rows, head * HD : (head + 1) * HD] = mixed[
                    first : first + rows
                ]
    for tile in range(tile_count):
        w_copies[tile].wait()
        out[:, tile * tile_width : (tile + 1) * tile_width] = jnp.dot(
            heads_buf[...], w_buf[tile], preferred_element_type=jnp.float32
        ).astype(jnp.bfloat16)


def project_rows(ticks, rows, place, arrays, deps):
    queries, new_kv, cache_kv, out_weight = arrays
    head_width = queries.shape[2]
    heads_here = head_width // HD
    kv_count = max(1, heads_here // GROUP)
    kv_width = kv_count * HD
    capacity = cache_kv.shape[1]
    columns = out_weight.shape[2]
    tile = min(COLUMN_TILE, columns)
    fresh_count = ticks[-1] + 1
    tick_count = len(ticks)
    all_rows = tick_count * (heads_here // kv_count) * rows
    anywhere = pl.BlockSpec(memory_space=pl.ANY)
    return pl.pallas_call(
        functools.partial(rows_kernel, ticks, rows, len(deps)),
        out_shape=jax.ShapeDtypeStruct((tick_count * rows, columns), jnp.bfloat16),
        in_specs=[pl.BlockSpec(memory_space=pltpu.SMEM)] + [anywhere] * (4 + len(deps)),
        out_specs=pl.BlockSpec(memory_space=pltpu.VMEM),
        scratch_shapes=[
            pltpu.VMEM((tick_count, rows, head_width), jnp.bfloat16),
            pltpu.VMEM((fresh_count, 2, queries.shape[1], kv_width), jnp.bfloat16),
            pltpu.VMEM((2, capacity, kv_width), jnp.bfloat16),
            pltpu.VMEM((columns // tile, head_width, tile), jnp.bfloat16),
            pltpu.VMEM((tick_count * rows, head_width), jnp.bfloat16),
            pltpu.VMEM((kv_count, all_rows, 2 * HD), jnp.float32),
            pltpu.SemaphoreType.DMA((tick_count + 2 * fresh_count + 2,)),
            pltpu.SemaphoreType.DMA((columns // tile,)),
        ],
        compiler_params=pltpu.CompilerParams(vmem_limit_bytes=40 * 2**20),
        cost_estimate=pl.CostEstimate(flops=1000, bytes_accessed=1000, transcendentals=0),
    )(place, queries, new_kv, cache_kv, out_weight, *deps)


def add(left, right):
    return (left.astype(jnp.float32) + right.astype(jnp.float32)).astype(jnp.bfloat16)


def on_device(residual, queries, new_kv, cache_kv, lengths, out_weight):
    section_count = lax.axis_size("section")
    head_count = lax.axis_size("head")
    section_index = lax.axis_index("section")
    z = lax.axis_index("head")
    tick_count, row_count, head_width = queries.shape
    heads_here = head_width // HD
    kv_column = (z * heads_here // GROUP) * HD
    my_length = lengths[section_index]
    arrays = (queries, new_kv, cache_kv, out_weight)
    rows = row_count // head_count
    ticks = tuple(range(tick_count))

    def place(row_first):
        return jnp.stack([row_first, my_length, kv_column]).astype(jnp.int32)

    def send(block, pairs, distance):
        route = [
            (s * head_count + a, (s + distance) % section_count * head_count + b)
            for s in range(section_count)
            for a, b in pairs
        ]
        return lax.ppermute(block, ("section", "head"), route)

    def by_tick(block):
        return block.reshape(tick_count, -1, block.shape[-1])

    if head_count != 4 or tick_count != 2:
        partial = project_rows(ticks, row_count, place(0 * z), arrays, ())
        pieces = [
            lax.psum_scatter(block, "head", scatter_dimension=0, tiled=True)
            for block in by_tick(partial)
        ]
        updated = add(residual, jnp.stack(pieces, axis=1))
        return send(updated, [(i, i) for i in range(head_count)], 1)

    ends = [(0, 1), (3, 2)]
    middle = [(1, 2), (2, 1)]
    outward = [(0, 1), (3, 2), (1, 0), (2, 3)]
    same = [(i, i) for i in range(head_count)]
    lower = z < 2
    is_end = (z == 0) | (z == 3)
    first = jnp.where(lower, 3, 0)
    second = jnp.where(lower, 2, 1)
    third = jnp.where(is_end, jnp.where(lower, 1, 2), jnp.where(lower, 0, 3))

    def pieces_of(chunk, ticks_now, deps):
        return project_rows(ticks_now, rows, place(chunk * rows), arrays, deps)

    a0 = pieces_of(first, (0,), ())
    a1 = pieces_of(first, (1,), (a0,))
    b0 = pieces_of(second, (0,), (a1,))
    b1 = pieces_of(second, (1,), (b0,))
    a0_far = send(a0, ends, 0)
    a1_far = send(a1, ends, 0)
    b0_far = send(b0, ends, 0)
    b1_far = send(b1, ends, 0)
    a0_sum = add(a0, a0_far)
    a0_mid = send(a0_sum, middle, 0)
    own = pieces_of(z, ticks, (b1, a0_sum))
    base = add(by_tick(own), residual.transpose(1, 0, 2))
    base_here = send(base, same, 1)
    a1_sum = add(a1, a1_far)
    a1_mid = send(a1_sum, middle, 0)
    c = pieces_of(third, ticks, (own, a1_sum))
    c_here = send(add(by_tick(c), jnp.stack([a0_mid, a1_mid])), outward, 1)
    b0_here = send(add(b0, b0_far), middle, 1)
    b1_here = send(add(b1, b1_far), middle, 1)
    total = (
        base_here.astype(jnp.float32)
        + c_here.astype(jnp.float32)
        + jnp.stack([b0_here, b1_here]).astype(jnp.float32)
    )
    return total.astype(jnp.bfloat16).transpose(1, 0, 2)


def solution(mesh):
    placed = (
        P(("section", "head"), None, None),
        P(None, "section", "head"),
        P(None, None, "section", None),
        P(None, "section", None),
        P(),
        P("section", "head", None),
    )
    return jax.shard_map(
        on_device,
        mesh=mesh,
        in_specs=placed,
        out_specs=P(("section", "head"), None, None),
        check_vma=False,
    )
```

time: 234 us -> 137 us (0.59)
  waiting for transfers between devices: 140 us -> 60.5 us
  Pallas kernels: 0 us -> 42.2 us
  matrix products: 37.7 us -> 0 us
  local copies, waits for them, and re-layouts: 31.1 us -> 11.8 us
  starting transfers between devices: 0.28 us -> 14.2 us
  between operations: 14.1 us -> 0.29 us
    reduce_scatter x2 -> x0, waiting for transfers between devices: 125 us -> none  [on_device(): lax.psum_scatter(project_rows(head_blocks[tick_now], weight_rows).astype(...]
    ppermute x1 -> x10, waiting for transfers between devices: 15.1 us -> 60.5 us  [send(): return lax.ppermute(block, ('section', 'head'), route)]
    pallas_call x0 -> x6, Pallas kernels: none -> 42.2 us  [project_rows(): pl.pallas_call(functools.partial(rows_kernel, ticks, rows, len(deps)), ou...]
    dot_general x16 -> x0, matrix products: 37.7 us -> none  [the longest x7 14.3 us: attend_block(): jnp.einsum('grk,gkd->grd', rounded, value_rows, preferred_element_type=jn...]
    ppermute x1 -> x10, starting transfers between devices: 0.06 us -> 14.2 us  [send(): return lax.ppermute(block, ('section', 'head'), route)]
    reshape x3 -> x0, local copies, waits for them, and re-layouts: 5.83 us -> none  [the longest x2 3.72 us: on_device(): queries.reshape(tick_count, row_count, kv_count, inner_count, HD)]
    while x20 -> x0, local copies, waits for them, and re-layouts: 5.37 us -> none
    dynamic_slice x2 -> x0, local copies, waits for them, and re-layouts: 3.51 us -> none  [the longest x1 2.65 us: on_device(): cache_part = lax.dynamic_slice_in_dim(cache_kv, kv_first * HD, kv_width, 2)]
  transfers between devices with their start and end apart: 3 -> 10, of which waited for: 3 -> 5; matrix products, arithmetic and copies ran while one was open for 5% -> 3% of each run, Pallas kernels for 0% -> 12%
where the time goes in v1:
time: 137 us; the launch traced here: 135 us
  waiting for transfers between devices  60.5 us (44%)
  Pallas kernels  42.2 us (31%)
  starting transfers between devices  14.2 us (10%)
  local copies, waits for them, and re-layouts  11.8 us (9%)
  other arithmetic  6.4 us (5%)
    ppermute x10, waiting for transfers between devices, send(): return lax.ppermute(block, ('section', 'head'), route)  60.5 us
    pallas_call x6, Pallas kernels, project_rows(): pl.pallas_call(functools.partial(rows_kernel, ticks, rows, len(deps)), ou...  42.2 us
    ppermute x10, starting transfers between devices, send(): return lax.ppermute(block, ('section', 'head'), route)  14.2 us
    unnamed x18, local copies, waits for them, and re-layouts  8.4 us
    convert_element_type x6, other arithmetic, add(): (left.astype(jnp.float32) + right.astype(jnp.float32)).astype(jnp.bfloat16)  3.68 us
  transfers between devices with their start and end apart: 10, of which 5 were waited for; matrix products, arithmetic and copies ran while one was open for 3% of the time, Pallas kernels for 12%

profile of v1, /device:TPU:16, one launch (start us, length us, event | category | flops | bytes accessed | tf_op | source)
XLA Modules:
  0.0 135.4 jit_solution(6107510339782919782)
XLA Ops:
  0.0 1.3 dynamic_slice.3
  1.3 0.7 add_add_fusion.2.place
  2.0 2.8 %copy-done = bf16[2,1536,1024]{2,1,0:T(8,128)(2,1)S(1)} copy-done((bf16[2,1536,1024]{2,1,0:T(8,128)(2,1)S(1)}, bf16[2,1536,1024]{2,1,0:T(8,128)(2,1)}, u32[]{:S(2)}) %copy-start) | copy-done | bytes 6291480
  4.8 1.6 %copy-done.2 = bf16[2,2,256,1024]{3,2,1,0:T(8,128)(2,1)S(1)} copy-done((bf16[2,2,256,1024]{3,2,1,0:T(8,128)(2,1)S(1)}, bf16[2,2,256,1024]{3,2,1,0:T(8,128)(2,1)}, u32[]{:S(2)}) %copy-start.2) | copy-done | bytes 2097176
  6.4 1.2 copy-done.4
  7.7 6.3 %shard_map.64.rest_0_ = bf16[64,4096]{1,0:T(8,128)(2,1)S(1)} custom-call(s32[3]{0:T(128)S(1)} %add_add_fusion.2.place, bf16[2,256,1024]{2,1,0:T(8,128)(2,1)S(1)} %copy-done.4, bf16[2,2,256,1024]{3,2,1,0:T(8,128)(2,1)S(1)} %copy-done.2, bf16[2,1536,1024]{2,1,0:T(8,128)(2,1)S(1)} %copy-done, bf16[1,1024,4096]{2,1,0:T(8,128)(2,1)} %out_weight.11), custom_call_target="tpu_custom_call" | custom-call | flops 1000 | bytes 1000 | tf_op jit(solution)/shard_map/pallas_call | solution.py:182
  13.9 0.7 add_add_fusion.1.place
  14.7 6.5 %shard_map.65.rest_0_ = bf16[64,4096]{1,0:T(8,128)(2,1)S(1)} custom-call(s32[3]{0:T(128)S(1)} %add_add_fusion.2.place, bf16[2,256,1024]{2,1,0:T(8,128)(2,1)S(1)} %copy-done.4, bf16[2,2,256,1024]{3,2,1,0:T(8,128)(2,1)S(1)} %copy-done.2, bf16[2,1536,1024]{2,1,0:T(8,128)(2,1)S(1)} %copy-done, bf16[1,1024,4096]{2,1,0:T(8,128)(2,1)} %out_weight.11, ...), custom_call_target="tpu_custom_call" | custom-call | flops 1000 | bytes 1000 | tf_op jit(solution)/shard_map/pallas_call | solution.py:182
  21.2 6.2 %shard_map.66.rest_0_ = bf16[64,4096]{1,0:T(8,128)(2,1)S(1)} custom-call(s32[3]{0:T(128)S(1)} %add_add_fusion.1.place, bf16[2,256,1024]{2,1,0:T(8,128)(2,1)S(1)} %copy-done.4, bf16[2,2,256,1024]{3,2,1,0:T(8,128)(2,1)S(1)} %copy-done.2, bf16[2,1536,1024]{2,1,0:T(8,128)(2,1)S(1)} %bitcast.18, bf16[1,1024,4096]{2,1,0:T(8,128)(2,1)} %out_weight.11, ...), custom_call_target="tpu_custom_call" | custom-call | flops 1000 | bytes 1000 | tf_op jit(solution)/shard_map/pallas_call | solution.py:182
  27.4 6.5 %shard_map.67.rest_0_ = bf16[64,4096]{1,0:T(8,128)(2,1)S(1)} custom-call(s32[3]{0:T(128)S(1)} %add_add_fusion.1.place, bf16[2,256,1024]{2,1,0:T(8,128)(2,1)S(1)} %copy-done.4, bf16[2,2,256,1024]{3,2,1,0:T(8,128)(2,1)S(1)} %copy-done.2, bf16[2,1536,1024]{2,1,0:T(8,128)(2,1)S(1)} %bitcast.18, bf16[1,1024,4096]{2,1,0:T(8,128)(2,1)} %out_weight.11, ...), custom_call_target="tpu_custom_call" | custom-call | flops 1000 | bytes 1000 | tf_op jit(solution)/shard_map/pallas_call | solution.py:182
  33.9 1.3 collective-permute-start.8
  35.2 1.3 collective-permute-start.6
  36.5 1.3 collective-permute-start.2
  37.8 1.3 collective-permute-start
  39.1 0.7 add_add_fusion
  39.9 10.9 %collective-permute-done.8 = bf16[64,4096]{1,0:T(8,128)(2,1)} collective-permute-done((bf16[64,4096]{1,0:T(8,128)(2,1)S(1)}, bf16[64,4096]{1,0:T(8,128)(2,1)}, u32[]{:S(2)}, u32[]{:S(2)}) %collective-permute-start.8) | collective-permute-done | bytes 524320 | tf_op jit(solution)/shard_map/ppermute | solution.py:228
  50.8 1.2 add_convert_fusion.1
  51.9 1.9 %collective-permute-start.9 = (bf16[64,4096]{1,0:T(8,128)(2,1)S(1)}, bf16[64,4096]{1,0:T(8,128)(2,1)S(1)}, u32[]{:S(2)}, u32[]{:S(2)}) collective-permute-start(bf16[64,4096]{1,0:T(8,128)(2,1)S(1)} %add_convert_fusion.1), channel_id=1, source_target_pairs={{1,6},{2,5},{5,10},{6,9},{9,14},{10,13},{13,18},{14,17},{17,22},{1... | collective-permute-start | bytes 1572872 | tf_op jit(solution)/shard_map/ppermute | solution.py:228
  53.9 18.3 %collective-permute-done.2 = bf16[64,4096]{1,0:T(8,128)(2,1)} collective-permute-done((bf16[64,4096]{1,0:T(8,128)(2,1)S(1)}, bf16[64,4096]{1,0:T(8,128)(2,1)}, u32[]{:S(2)}, u32[]{:S(2)}) %collective-permute-start.2) | collective-permute-done | bytes 524320 | tf_op jit(solution)/shard_map/ppermute | solution.py:228
  72.1 1.2 add_convert_fusion.3.rest_1_
  73.3 2.4 %collective-permute-start.4 = (bf16[64,4096]{1,0:T(8,128)(2,1)S(1)}, bf16[64,4096]{1,0:T(8,128)(2,1)S(1)}, u32[]{:S(2)}, u32[]{:S(2)}) collective-permute-start(bf16[64,4096]{1,0:T(8,128)(2,1)S(1)} %add_convert_fusion.3.rest_1_), channel_id=1, source_target_pairs={{1,2},{2,1},{5,6},{6,5},{9,10},{10,9},{13,14},{14,13},{17,18},{18,... | collective-permute-start | bytes 1572872 | tf_op jit(solution)/shard_map/ppermute | solution.py:228
  75.7 2.0 %collective-permute-done = bf16[64,4096]{1,0:T(8,128)(2,1)S(1)} collective-permute-done((bf16[64,4096]{1,0:T(8,128)(2,1)S(1)}, bf16[64,4096]{1,0:T(8,128)(2,1)S(1)}, u32[]{:S(2)}, u32[]{:S(2)}) %collective-permute-start) | collective-permute-done | bytes 524320 | tf_op jit(solution)/shard_map/ppermute | solution.py:228
  77.8 2.5 %collective-permute-start.3 = (bf16[64,4096]{1,0:T(8,128)(2,1)S(1)}, bf16[64,4096]{1,0:T(8,128)(2,1)S(1)}, u32[]{:S(2)}, u32[]{:S(2)}) collective-permute-start(bf16[64,4096]{1,0:T(8,128)(2,1)S(1)} %add_convert_fusion.4.rest_1_), channel_id=1, source_target_pairs={{1,2},{2,1},{5,6},{6,5},{9,10},{10,9},{13,14},{14,13},{17,18},{18,... | collective-permute-start | bytes 1572872 | tf_op jit(solution)/shard_map/ppermute | solution.py:228
  80.4 2.8 %copy-done.1 = bf16[2,1536,1024]{2,1,0:T(8,128)(2,1)S(1)} copy-done((bf16[2,1536,1024]{2,1,0:T(8,128)(2,1)S(1)}, bf16[2,1536,1024]{2,1,0:T(8,128)(2,1)}, u32[]{:S(2)}) %copy-start.1) | copy-done | bytes 6291480
  83.1 8.4 %shard_map.68.rest_0_ = bf16[128,4096]{1,0:T(8,128)(2,1)S(1)} custom-call(s32[3]{0:T(128)S(1)} %get-tuple-element.5.place, bf16[2,256,1024]{2,1,0:T(8,128)(2,1)S(1)} %copy-done.5, bf16[2,2,256,1024]{3,2,1,0:T(8,128)(2,1)S(1)} %copy-done.3, bf16[2,1536,1024]{2,1,0:T(8,128)(2,1)S(1)} %copy-done.1, bf16[1,1024,4096]{2,1,0:T(8,128)(2,1)} %out_weight.11, ...), custom_call_target="tpu_custom_call" | custom-call | flops 1000 | bytes 1000 | tf_op jit(solution)/shard_map/pallas_call | solution.py:182
  91.5 8.4 %shard_map.69 = bf16[128,4096]{1,0:T(8,128)(2,1)S(1)} custom-call(s32[3]{0:T(128)S(1)} %get-tuple-element.6.place, bf16[2,256,1024]{2,1,0:T(8,128)(2,1)S(1)} %copy-done.5, bf16[2,2,256,1024]{3,2,1,0:T(8,128)(2,1)S(1)} %copy-done.3, bf16[2,1536,1024]{2,1,0:T(8,128)(2,1)S(1)} %copy-done.1, bf16[1,1024,4096]{2,1,0:T(8,128)(2,1)} %out_weight.11, ...), custom_call_target="tpu_custom_call" | custom-call | flops 1000 | bytes 1000 | tf_op jit(solution)/shard_map/pallas_call | solution.py:182
  99.9 0.9 fusion.1
  101.3 2.1 %collective-permute-start.7 = (bf16[64,4096]{1,0:T(8,128)(2,1)S(1)}, bf16[64,4096]{1,0:T(8,128)(2,1)S(1)}, u32[]{:S(2)}, u32[]{:S(2)}) collective-permute-start(bf16[64,4096]{1,0:T(8,128)(2,1)S(1)} %add_convert_fusion.2), channel_id=1, source_target_pairs={{1,6},{2,5},{5,10},{6,9},{9,14},{10,13},{13,18},{14,17},{17,22},{1... | collective-permute-start | bytes 1572872 | tf_op jit(solution)/shard_map/ppermute | solution.py:228
  103.4 15.6 %collective-permute-done.7 = bf16[64,4096]{1,0:T(8,128)(2,1)S(1)} collective-permute-done((bf16[64,4096]{1,0:T(8,128)(2,1)S(1)}, bf16[64,4096]{1,0:T(8,128)(2,1)S(1)}, u32[]{:S(2)}, u32[]{:S(2)}) %collective-permute-start.7) | collective-permute-done | bytes 524320 | tf_op jit(solution)/shard_map/ppermute | solution.py:228
  119.0 13.8 %collective-permute-done.1 = bf16[2,64,4096]{2,1,0:T(8,128)(2,1)S(1)} collective-permute-done((bf16[2,64,4096]{2,1,0:T(8,128)(2,1)S(1)}, bf16[2,64,4096]{2,1,0:T(8,128)(2,1)S(1)}, u32[]{:S(2)}, u32[]{:S(2)}) %collective-permute-start.1) | collective-permute-done | bytes 1048608 | tf_op jit(solution)/shard_map/ppermute | solution.py:228
  132.8 0.5 fusion.2
  133.3 2.1 %copy.8 = bf16[64,2,4096]{2,1,0:T(2,128)(2,1)} copy(bf16[64,2,4096]{2,0,1:T(8,128)(2,1)S(1)} %fusion.2) | data formatting | bytes 2097152 | tf_op jit(solution)/shard_map/transpose | solution.py:279
  (25 shorter events, 0.7 us)
Async XLA Ops:
  2.0 2.8 %copy-start = (bf16[2,1536,1024]{2,1,0:T(8,128)(2,1)S(1)}, bf16[2,1536,1024]{2,1,0:T(8,128)(2,1)}, u32[]{:S(2)}) copy-start(bf16[2,1536,1024]{2,1,0:T(8,128)(2,1)} %cache_kv.11) | copy-start | bytes 18874372
  4.8 1.6 %copy-start.2 = (bf16[2,2,256,1024]{3,2,1,0:T(8,128)(2,1)S(1)}, bf16[2,2,256,1024]{3,2,1,0:T(8,128)(2,1)}, u32[]{:S(2)}) copy-start(bf16[2,2,256,1024]{3,2,1,0:T(8,128)(2,1)} %new_kv.11) | copy-start | bytes 6291460
  6.4 1.2 copy-start.4
  7.7 13.5 %slice-start = ((s8[6291456]{0:T(1024)(128)(4,1)}), s8[4194304]{0:T(1024)(128)(4,1)S(1)}, s32[]{:S(2)}) async-start(s8[6291456]{0:T(1024)(128)(4,1)} %bitcast.17), calls=%async_computation | async-start | bytes 8388608
  14.7 6.5 %slice-start.1 = ((s8[6291456]{0:T(1024)(128)(4,1)}), s8[2097152]{0:T(1024)(128)(4,1)S(1)}, s32[]{:S(2)}) async-start(s8[6291456]{0:T(1024)(128)(4,1)} %bitcast.17), calls=%async_computation.1 | async-start | bytes 4194304
  33.9 16.9 %collective-permute-start.8 = (bf16[64,4096]{1,0:T(8,128)(2,1)S(1)}, bf16[64,4096]{1,0:T(8,128)(2,1)}, u32[]{:S(2)}, u32[]{:S(2)}) collective-permute-start(bf16[64,4096]{1,0:T(8,128)(2,1)S(1)} %shard_map.67.rest_0_), channel_id=1, source_target_pairs={{0,1},{3,2},{4,5},{7,6},{8,9},{11,10},{12,13},{15,14},{16,17},{19,... | collective-permute-start | bytes 1572872 | tf_op jit(solution)/shard_map/ppermute | solution.py:228
  35.2 66.0 %collective-permute-start.6 = (bf16[64,4096]{1,0:T(8,128)(2,1)S(1)}, bf16[64,4096]{1,0:T(8,128)(2,1)S(1)}, u32[]{:S(2)}, u32[]{:S(2)}) collective-permute-start(bf16[64,4096]{1,0:T(8,128)(2,1)S(1)} %shard_map.66.rest_0_), channel_id=1, source_target_pairs={{0,1},{3,2},{4,5},{7,6},{8,9},{11,10},{12,13},{15,14},{16,17},{19,... | collective-permute-start | bytes 1572872 | tf_op jit(solution)/shard_map/ppermute | solution.py:228
  36.5 35.6 %collective-permute-start.2 = (bf16[64,4096]{1,0:T(8,128)(2,1)S(1)}, bf16[64,4096]{1,0:T(8,128)(2,1)}, u32[]{:S(2)}, u32[]{:S(2)}) collective-permute-start(bf16[64,4096]{1,0:T(8,128)(2,1)S(1)} %shard_map.65.rest_0_), channel_id=1, source_target_pairs={{0,1},{3,2},{4,5},{7,6},{8,9},{11,10},{12,13},{15,14},{16,17},{19,... | collective-permute-start | bytes 1572872 | tf_op jit(solution)/shard_map/ppermute | solution.py:228
  37.8 39.8 %collective-permute-start = (bf16[64,4096]{1,0:T(8,128)(2,1)S(1)}, bf16[64,4096]{1,0:T(8,128)(2,1)S(1)}, u32[]{:S(2)}, u32[]{:S(2)}) collective-permute-start(bf16[64,4096]{1,0:T(8,128)(2,1)S(1)} %shard_map.64.rest_0_), channel_id=1, source_target_pairs={{0,1},{3,2},{4,5},{7,6},{8,9},{11,10},{12,13},{15,14},{16,17},{19,... | collective-permute-start | bytes 1572872 | tf_op jit(solution)/shard_map/ppermute | solution.py:228
  39.9 40.5 %copy-start.3 = (bf16[2,2,256,1024]{3,2,1,0:T(8,128)(2,1)S(1)}, bf16[2,2,256,1024]{3,2,1,0:T(8,128)(2,1)}, u32[]{:S(2)}) copy-start(bf16[2,2,256,1024]{3,2,1,0:T(8,128)(2,1)} %new_kv.11) | copy-start | bytes 6291460
  39.9 40.5 %copy-start.5 = (bf16[2,256,1024]{2,1,0:T(8,128)(2,1)S(1)}, bf16[2,256,1024]{2,1,0:T(8,128)(2,1)}, u32[]{:S(2)}) copy-start(bf16[2,256,1024]{2,1,0:T(8,128)(2,1)} %queries.11) | copy-start | bytes 3145732
  51.9 51.5 %collective-permute-start.9 = (bf16[64,4096]{1,0:T(8,128)(2,1)S(1)}, bf16[64,4096]{1,0:T(8,128)(2,1)S(1)}, u32[]{:S(2)}, u32[]{:S(2)}) collective-permute-start(bf16[64,4096]{1,0:T(8,128)(2,1)S(1)} %add_convert_fusion.1), channel_id=1, source_target_pairs={{1,6},{2,5},{5,10},{6,9},{9,14},{10,13},{13,18},{14,17},{17,22},{1... | collective-permute-start | bytes 1572872 | tf_op jit(solution)/shard_map/ppermute | solution.py:228
  73.3 27.5 %collective-permute-start.4 = (bf16[64,4096]{1,0:T(8,128)(2,1)S(1)}, bf16[64,4096]{1,0:T(8,128)(2,1)S(1)}, u32[]{:S(2)}, u32[]{:S(2)}) collective-permute-start(bf16[64,4096]{1,0:T(8,128)(2,1)S(1)} %add_convert_fusion.3.rest_1_), channel_id=1, source_target_pairs={{1,2},{2,1},{5,6},{6,5},{9,10},{10,9},{13,14},{14,13},{17,18},{18,... | collective-permute-start | bytes 1572872 | tf_op jit(solution)/shard_map/ppermute | solution.py:228
  77.8 23.1 %collective-permute-start.3 = (bf16[64,4096]{1,0:T(8,128)(2,1)S(1)}, bf16[64,4096]{1,0:T(8,128)(2,1)S(1)}, u32[]{:S(2)}, u32[]{:S(2)}) collective-permute-start(bf16[64,4096]{1,0:T(8,128)(2,1)S(1)} %add_convert_fusion.4.rest_1_), channel_id=1, source_target_pairs={{1,2},{2,1},{5,6},{6,5},{9,10},{10,9},{13,14},{14,13},{17,18},{18,... | collective-permute-start | bytes 1572872 | tf_op jit(solution)/shard_map/ppermute | solution.py:228
  80.3 2.8 %copy-start.1 = (bf16[2,1536,1024]{2,1,0:T(8,128)(2,1)S(1)}, bf16[2,1536,1024]{2,1,0:T(8,128)(2,1)}, u32[]{:S(2)}) copy-start(bf16[2,1536,1024]{2,1,0:T(8,128)(2,1)} %cache_kv.11) | copy-start | bytes 18874372
  91.5 8.4 %copy-start.6 = (bf16[64,2,4096]{2,1,0:T(2,128)(2,1)S(1)}, bf16[64,2,4096]{2,1,0:T(2,128)(2,1)}, u32[]{:S(2)}) copy-start(bf16[64,2,4096]{2,1,0:T(2,128)(2,1)} %param.6) | copy-start | bytes 3145732
  100.8 32.0 %collective-permute-start.1 = (bf16[2,64,4096]{2,1,0:T(8,128)(2,1)S(1)}, bf16[2,64,4096]{2,1,0:T(8,128)(2,1)S(1)}, u32[]{:S(2)}, u32[]{:S(2)}) collective-permute-start(bf16[2,64,4096]{2,1,0:T(8,128)(2,1)S(1)} %fusion.1), channel_id=1, source_target_pairs={{0,4},{1,5},{2,6},{3,7},{4,8},{5,9},{6,10},{7,11},{8,12},{9,13},{1... | collective-permute-start | bytes 3145736 | tf_op jit(solution)/shard_map/ppermute | solution.py:228
  101.1 31.7 %collective-permute-start.5 = (bf16[2,64,4096]{2,1,0:T(8,128)(2,1)S(1)}, bf16[2,64,4096]{2,1,0:T(8,128)(2,1)S(1)}, u32[]{:S(2)}, u32[]{:S(2)}) collective-permute-start(bf16[2,64,4096]{2,1,0:T(8,128)(2,1)S(1)} %fusion), channel_id=1, source_target_pairs={{0,5},{3,6},{1,4},{2,7},{4,9},{7,10},{5,8},{6,11},{8,13},{11,14},{... | collective-permute-start | bytes 3145736 | tf_op jit(solution)/shard_map/ppermute | solution.py:228
  101.3 17.7 %collective-permute-start.7 = (bf16[64,4096]{1,0:T(8,128)(2,1)S(1)}, bf16[64,4096]{1,0:T(8,128)(2,1)S(1)}, u32[]{:S(2)}, u32[]{:S(2)}) collective-permute-start(bf16[64,4096]{1,0:T(8,128)(2,1)S(1)} %add_convert_fusion.2), channel_id=1, source_target_pairs={{1,6},{2,5},{5,10},{6,9},{9,14},{10,13},{13,18},{14,17},{17,22},{1... | collective-permute-start | bytes 1572872 | tf_op jit(solution)/shard_map/ppermute | solution.py:228
